TPU v7x, 32 devices: a whole 2x2x4 slice. The times are simulated.
32 devices in a mesh: feat: 8 (over z, y), cls: 4 (over x, core).
Axes of the slice: x: 2, y: 2, z: 4, core: 2. Of those that a mesh axis runs over, the one named last changes fastest.
Arguments:
- inputs: bfloat16 [2, 1024, 360], P(None, 'feat'), may hold values from -6 to 6
- projection: bfloat16 [360, 65536], P(None, 'feat'), may hold values from -0.3125 to 0.3125
- offsets: int32 [65536], P('feat'), may hold values from 0 to 65520
- labels: int32 [2, 1024], replicated, may hold values from 0 to 4999
- weights: float32 [65536, 5000], P('feat', 'cls'), may hold values from -6 to 6
Outputs:
- updated_weights: float32 [65536, 5000], P('feat', 'cls')
- losses: float32 [2], replicated
All inputs are finite; a program needn't handle non-finite values.
Results may differ from a plain program's by a relative error of at most 0.00061.
Values may be sent and summed in bfloat16 or wider, within the bound.
No kernel may reach another device: no remote copies, remote signals or barrier semaphores. Data moves between devices by JAX's collectives and lax.ppermute only.
A program may use at most 192 MiB of HBM per device.

v0:
```python
import functools
import math

import jax
import jax.numpy as jnp
from jax import lax
from jax.experimental import pallas as pl
from jax.experimental.pallas import tpu as pltpu
from jax.sharding import PartitionSpec as P

f32, bf16 = jnp.float32, jnp.bfloat16
learning_rate = 10.0
VMEM_LIMIT = 44 * 1024 * 1024
S0, S1, S2, S3 = 6.283164044274001, -41.33714236744706, 81.34076877058536, -70.99343220053879
NT = (((1,), (1,)), ((), ()))


def features_of(x, p, turns, scale):
    u = jnp.dot(x, p, preferred_element_type=f32) * (0.5 / math.pi) + turns
    t = jnp.abs(u - jnp.round(u)) - 0.25
    s = t * t
    return (t * (scale * S0 + s * (scale * S1 + s * (scale * S2 + s * (scale * S3))))).astype(bf16)


def after_specs(after):
    return [pl.BlockSpec(memory_space=pl.ANY)] * len(after)


def scores_kernel(steps, scale, first, extra, count, skip, given, *refs):
    where_ref, xs, refs = refs[0], refs[1 : 1 + given], refs[1 + given :]
    p_ref, off_ref, w_ref, refs = refs[0], refs[1], refs[2], refs[3:]
    if extra:
        e_ref, refs = refs[0], refs[1:]
    if first:
        pair, refs = refs[:2], refs[2:]
    refs = refs[skip:]
    f_ref, send_ref, keep_ref, refs = refs[0], refs[1], refs[2], refs[3:]
    if first:
        narrow_ref, stack_ref, refs = refs[0], refs[1], refs[2:]
    x_ref, last_ref, acc_ref = refs
    j = pl.program_id(0)
    fr = send_ref.shape[2]
    rows = acc_ref.shape[1] - (2 * fr if extra else 0)
    groups = acc_ref.shape[0]

    @pl.when(j == 0)
    def _():
        for k in range(2 * groups):
            x_ref[k * fr : (k + 1) * fr, :] = (xs[k][...] if given == 2 * groups else xs[k // 2][k % 2]).T
        if first:
            for k in range(2):
                stack_ref[k] = pair[k][...]
        acc_ref[...] = jnp.zeros(acc_ref.shape, f32)

    def features(k):
        at = pl.ds(k * fr, fr)
        turns = off_ref[...].astype(f32) * (1.0 / 65521.0)
        f_ref[at, :] = features_of(x_ref[at, :], p_ref[...], turns, scale)

    def scores(k):
        g, part = k // 2, k % 2
        x = last_ref[g * 2 * fr : (g + 1) * 2 * fr, :]
        if first and k == 0:
            narrow_ref[0:count, :] = w_ref[...].astype(bf16)
            narrow_ref[count:, :] = jnp.zeros((rows - count, narrow_ref.shape[1]), bf16)
        w = narrow_ref if first else w_ref
        cut = (rows + (2 * fr if extra else 0)) // 32 * 16
        at = slice(0, cut) if part == 0 else slice(cut, rows)
        left = w[at, :]
        if extra and part == 1:
            at, left = slice(cut, rows + 2 * fr), jnp.concatenate([left, e_ref[...]], axis=0)
        acc_ref[g, at, :] += lax.dot_general(left, x, NT, preferred_element_type=f32)

    @pl.when(j == 0)
    def _():
        for k in range(2 * groups):
            features(k)

    @pl.when(j == 0)
    def _():
        last_ref[...] = f_ref[...]

    @pl.when((j > 0) & (j < steps))
    def _():
        for k in range(2 * groups):
            scores(k)
            features(k)
        last_ref[...] = f_ref[...]

    @pl.when(j == steps)
    def _():
        for k in range(2 * groups):
            scores(k)
        for g in range(groups):
            if extra:
                low, high = acc_ref[g, rows : rows + fr, :], acc_ref[g, rows + fr :, :]
                acc_ref[g, rows : rows + fr, :] = jnp.where(where_ref[1] == 0, low, high)
                acc_ref[g, rows + fr :, :] = jnp.where(where_ref[1] == 0, high, low)
            keep_ref[g] = acc_ref[g, :, :fr]
            send_ref[g] = acc_ref[g, :, fr:].astype(bf16)


def scores_call(where, groups, at, xs, projection, turns, w, count, scale, earlier, pair=None, extra=None, after=(), fb=1024):
    din, nf = projection.shape
    fr = xs[0].shape[-1]
    rows, steps = -(-count // 16) * 16, nf // fb
    first = pair is not None
    total_rows = rows + (2 * fr if extra is not None else 0)
    now = lambda j, w: (0, jnp.minimum(j, steps - 1))
    last = lambda j, w: (0, jnp.maximum(j - 1, 0))
    in_specs = [whole(x.shape) for x in xs] + [
        pl.BlockSpec((din, fb), now),
        pl.BlockSpec((1, fb), now),
        pl.BlockSpec((count if first else rows, fb), last),
    ]
    operands = [where, *xs, projection, turns, w]
    if extra is not None:
        in_specs.append(pl.BlockSpec((2 * fr, fb), lambda j, w: (3 - (w[3] ^ w[2]), jnp.maximum(j - 1, 0))))
        operands.append(extra)
    if first:
        in_specs += [whole(p.shape) for p in pair]
        operands += pair
    unused = [] if earlier is None else [earlier]
    alias = {} if earlier is None else {len(operands): 0}
    unused += after
    in_specs += after_specs(unused)
    operands += unused
    outs = [((8 * fr, nf), bf16), ((groups, total_rows, fr), bf16), ((groups, total_rows, fr), f32)]
    out_specs = [
        pl.BlockSpec((2 * groups * fr, fb), lambda j, w: (at, jnp.minimum(j, steps - 1))),
        whole((groups, total_rows, fr)),
        whole((groups, total_rows, fr)),
    ]
    if first:
        outs += [((rows, nf), bf16), ((2, din, fr), bf16)]
        out_specs += [pl.BlockSpec((rows, fb), last), whole((2, din, fr))]
    return pl.pallas_call(
        functools.partial(scores_kernel, steps, scale, first, extra is not None, count, len(unused), len(xs)),
        grid_spec=pltpu.PrefetchScalarGridSpec(
            num_scalar_prefetch=1,
            grid=(steps + 1,),
            in_specs=in_specs,
            out_specs=out_specs,
            scratch_shapes=[
                pltpu.VMEM((2 * groups * fr, din), bf16),
                pltpu.VMEM((2 * groups * fr, fb), bf16),
                pltpu.VMEM((groups, total_rows, 2 * fr), f32),
            ],
        ),
        out_shape=[jax.ShapeDtypeStruct(s, d) for s, d in outs],
        input_output_aliases=alias,
        compiler_params=pltpu.CompilerParams(vmem_limit_bytes=VMEM_LIMIT),
        cost_estimate=pl.CostEstimate(
            flops=4 * groups * fr * nf * (din + total_rows), bytes_accessed=nf * (2 * rows + 4 * groups * fr), transcendentals=0
        ),
        name="features_scores",
    )(*operands)


def whole(shape):
    return pl.BlockSpec(shape, lambda *a: (0,) * len(shape))


def small_call(kernel, where, operands, outs, name, scratch=(), after=(), carry=()):
    n, m = 1 + len(operands), len(outs)

    def body(*refs):
        rest = refs[n + len(after) + len(carry) :]
        kernel(*refs[:n], *rest[:m], *rest[m + len(carry) :])

    return pl.pallas_call(
        body,
        grid_spec=pltpu.PrefetchScalarGridSpec(
            num_scalar_prefetch=1,
            grid=(1,),
            in_specs=[whole(o.shape) for o in operands] + after_specs([*after, *carry]),
            out_specs=[whole(s) for s, _ in outs] + after_specs(carry),
            scratch_shapes=list(scratch),
        ),
        out_shape=[jax.ShapeDtypeStruct(s, d) for s, d in outs] + [jax.ShapeDtypeStruct(c.shape, c.dtype) for c in carry],
        input_output_aliases={n + len(after) + i: m + i for i in range(len(carry))},
        compiler_params=pltpu.CompilerParams(vmem_limit_bytes=24 * 1024 * 1024),
        cost_estimate=pl.CostEstimate(flops=0, bytes_accessed=8_000_000, transcendentals=0),
        name=name,
    )(where, *operands, *after, *carry)


def sums_kernel(where_ref, keep_ref, got_ref, *outs):
    for k, out in enumerate(outs):
        out[...] = (keep_ref[k] + got_ref[k].astype(f32)).astype(out.dtype)


def swap(x, k):
    return lax.ppermute(x, "feat", [(i, i ^ k) for i in range(8)])


def pair_sums(where, keep, got, types, after=(), carry=()):
    s = keep.shape[1:]
    return small_call(sums_kernel, where, [keep, got], [(s, t) for t in types], "pair_sums", (), after, carry)


def over_cls(x):
    return [x] + [lax.ppermute(x, "cls", [(i, i ^ k) for i in range(4)]) for k in (1, 2, 3)]


def total(parts):
    parts = [p.astype(f32) for p in parts]
    return functools.reduce(lambda a, b: a + b, parts[1:], parts[0])


def part_rows(ref, at):
    return ref[0, at, :] if len(ref.shape) == 3 else ref[at, :]


def gram_kernel(where_ref, *refs):
    out = refs[-1]
    rows = out.shape[0]
    out[...] = total([part_rows(p, pl.ds(p.shape[-2] - rows, rows)) for p in refs[:-1]]).astype(bf16)


def target_kernel(count, given, second, where_ref, *refs):
    parts, lab_ref, refs = refs[:given], refs[given], refs[given + 1 :]
    if second:
        gram, grads, refs = refs[:4], refs[4:8], refs[8:]
    s_ref, t_ref, refs = refs[0], refs[1], refs[2:]
    rows, fr = s_ref.shape
    s_ref[...] = total([part_rows(r, slice(0, rows)) for r in parts])
    if second:
        fi, q = where_ref[0], where_ref[2]
        gram_ref = refs[0]
        quarter = gram[0].shape[0]
        for k in range(4):
            at = pl.ds(pl.multiple_of((q ^ k) * quarter, quarter), quarter)
            gram_ref[at, :] = gram[k][...]
        change = jnp.zeros((rows, fr), f32)
        for k in range(8):
            at = pl.ds(pl.multiple_of((fi ^ k) * fr, fr), fr)
            change += jnp.dot(block_of(grads, k), gram_ref[at, :], preferred_element_type=f32)
        s_ref[...] -= learning_rate * change
    row = lax.broadcasted_iota(jnp.int32, s_ref.shape, 0)
    is_target = (row + where_ref[2] * count == lab_ref[...]) & (row < count)
    t_ref[...] = jnp.sum(jnp.where(is_target, s_ref[...], 0.0), axis=0, keepdims=True)


def margin_kernel(count, classes, where_ref, s_ref, lab_ref, target_ref, slope_ref, sums_ref):
    row = lax.broadcasted_iota(jnp.int32, s_ref.shape, 0)
    valid = row < count
    is_target = row + where_ref[2] * count == lab_ref[...]
    margin = jnp.where(valid & ~is_target, jnp.maximum(0.0, 1.0 + s_ref[...] - target_ref[...]), 0.0)
    slope = 2.0 * margin / (classes - 1)
    slope_ref[...] = slope
    sums_ref[0:1, :] = jnp.sum(slope, axis=0, keepdims=True)
    sums_ref[1:2, :] = jnp.sum(margin * margin, axis=0, keepdims=True) / (classes - 1)


def grad_kernel(count, where_ref, slope_ref, lab_ref, sums_ref, g_ref):
    row = lax.broadcasted_iota(jnp.int32, slope_ref.shape, 0)
    is_target = (row + where_ref[2] * count == lab_ref[...]) & (row < count)
    value = jnp.where(is_target, -sums_ref[0:1, :], slope_ref[...])
    rest = sums_ref[1:2, :]
    for n in range(3):
        term = rest.astype(bf16).astype(f32)
        value = jnp.where(row == count + n, term, value)
        rest = rest - term
    g_ref[...] = value.astype(bf16)


def stack_kernel(where_ref, a_ref, b_ref, c_ref, out_ref):
    for k, r in enumerate((a_ref, b_ref, c_ref)):
        out_ref[k] = r[...]


def spread(where, block, after, carry=()):
    line = [swap(block, k) for k in (2, 4, 6)]
    pair = swap(block, 1)
    line, *carry = small_call(stack_kernel, where, line, [((3, *block.shape), bf16)], "line", (), after, carry)
    return [block, pair, line, swap(line, 1)], *carry


def block_of(grads, k):
    return grads[k][...] if k < 2 else grads[2 + k % 2][k // 2 - 1]


def update_kernel(count, skip, first, where_ref, *refs):
    grads, refs = refs[:4], refs[4:]
    f_ref, w_ref, refs = refs[0], refs[1], refs[2:]
    if not first:
        refs0, refs = refs[0], refs[1:]
    refs = refs[skip:]
    out_ref, loss_ref, g_ref = refs
    fr = grads[0].shape[1]

    @pl.when(pl.program_id(0) == 0)
    def _():
        losses = jnp.zeros((8, fr), f32)
        place = lax.broadcasted_iota(jnp.int32, losses.shape, 0)
        for k in range(8):
            g = block_of(grads, k)
            at = 6 - k // 2 * 2 + k % 2
            g_ref[:, at * fr : (at + 1) * fr] = g
            loss = sum(g[count + n : count + n + 1, :].astype(f32) for n in range(3))
            losses = jnp.where(place == (where_ref[0] ^ k), loss, losses)
        losses = jnp.sum(losses)
        if first:
            loss_ref[...] = jnp.zeros(loss_ref.shape, f32) + losses
        else:
            lane = lax.broadcasted_iota(jnp.int32, loss_ref.shape, 1)
            loss_ref[...] = jnp.where(lane == 0, refs0[...], losses)

    change = jnp.dot(g_ref[...], f_ref[...], preferred_element_type=f32)
    out_ref[...] = w_ref[...] - learning_rate * change[: out_ref.shape[0]]


def update_call(where, grads, features, wt, earlier=None, part=(0, 1), after=(), loss=None, fb=1024):
    frames, nf = features.shape
    rows, fr = grads[0].shape
    count = wt.shape[0]
    steps = nf // fb // part[1]
    begin = part[0] * steps
    spec = pl.BlockSpec((count, fb), lambda j, w: (0, begin + j))
    alias = {}
    if earlier is wt:
        alias = {6: 0}
    elif earlier is not None:
        alias = {7 if loss is None else 8: 0}
        after = [earlier, *after]
    return pl.pallas_call(
        functools.partial(update_kernel, count, len(after), loss is None),
        grid_spec=pltpu.PrefetchScalarGridSpec(
            num_scalar_prefetch=1,
            grid=(steps,),
            in_specs=[whole(g.shape) for g in grads]
            + [pl.BlockSpec((frames, fb), lambda j, w: (0, begin + j)), spec]
            + [whole((1, 2)) for x in [loss] if x is not None]
            + after_specs(after),
            out_specs=[spec, whole((1, 2))],
            scratch_shapes=[pltpu.VMEM((rows, frames), bf16)],
        ),
        out_shape=[jax.ShapeDtypeStruct(wt.shape, f32), jax.ShapeDtypeStruct((1, 2), f32)],
        input_output_aliases=alias,
        compiler_params=pltpu.CompilerParams(vmem_limit_bytes=VMEM_LIMIT),
        cost_estimate=pl.CostEstimate(
            flops=2 * frames * steps * fb * rows, bytes_accessed=steps * fb * (8 * rows + 2 * frames), transcendentals=0
        ),
        name="update",
    )(where, *grads, features, wt, *([] if loss is None else [loss]), *after)


def per_device(nfeat, ncls, inputs, projection, offsets, labels, weights):
    fi, q = lax.axis_index("feat"), lax.axis_index("cls")
    where = jnp.stack([fi, fi & 1, q, fi >> 1]).astype(jnp.int32)
    scale = math.sqrt(2.0 / nfeat)
    wt = weights.T
    xt = jnp.swapaxes(inputs, 1, 2)
    fr = xt.shape[2]
    count = wt.shape[0]
    rows = -(-count // 16) * 16
    turns = offsets.reshape(1, -1)
    own_labels = lax.dynamic_slice_in_dim(labels, fi * fr, fr, 1)

    def step(p, parts, extra, after=(), carry=()):
        lab = own_labels[p : p + 1]
        shape = (rows, fr)
        scratch = [pltpu.VMEM((8 * fr, fr), bf16)] if extra else []
        s, t, *carry = small_call(
            functools.partial(target_kernel, count, len(parts), bool(extra)),
            where,
            [*parts, lab, *extra],
            [(shape, f32), ((1, fr), f32)],
            "target",
            scratch,
            after,
            carry,
        )
        slope, sums = small_call(
            functools.partial(margin_kernel, count, ncls),
            where,
            [s, lab, lax.psum(t, "cls")],
            [(shape, f32), ((2, fr), f32)],
            "margin",
        )
        (g,) = small_call(
            functools.partial(grad_kernel, count),
            where,
            [slope, lab, lax.psum(sums, "cls")],
            [(shape, bf16)],
            "step_grad",
        )
        return g, *carry

    x = [xt[0]] + [swap(xt[0], k) for k in range(1, 8)]
    other = swap(xt[1], 1)
    f1, send_b, keep_b, narrow, pair = scores_call(
        where, 3, 0, x[6:8] + x[4:6] + x[2:4], projection, turns, wt, count, scale, None, [xt[1], other]
    )
    got_b = swap(send_b, 1)
    pairs = [swap(pair, 2 * k) for k in (3, 2, 1)] + [pair]
    f1, send_o, keep_o = scores_call(where, 1, 3, x[:2], projection, turns, narrow, count, scale, f1)
    *sums, send_o = pair_sums(where, keep_b, got_b, [bf16] * 3, [keep_o, *pairs], [send_o])
    parts = [keep_o, swap(send_o, 1)] + [swap(r, k) for r, k in zip(sums, (6, 4, 2))]
    f2, send_f, keep_f = scores_call(
        where, 2, 0, pairs[:2], projection, turns, narrow, count, scale, None, None, f1, [sums[0]]
    )
    g1, send_f = step(0, parts, [], [keep_f], [send_f])
    got_f = swap(send_f, 1)
    r3, r2 = pair_sums(where, keep_f, got_f, [bf16] * 2, [g1])
    f2, send_n, keep_n = scores_call(
        where, 2, 1, pairs[2:], projection, turns, narrow, count, scale, f2, None, f1, [r2]
    )
    r3, r2 = swap(r3, 6), swap(r2, 4)
    all1, send_n = spread(where, g1, [keep_n], [send_n])
    r1, own = pair_sums(where, keep_n, swap(send_n, 1), [bf16, f32], [all1[2]])
    parts = [own, swap(r1, 2), r2, r3]
    (gram,) = small_call(gram_kernel, where, parts, [((2 * fr, fr), bf16)], "gram")
    (g2,) = step(1, parts, [*over_cls(gram), *all1])
    w1, loss1 = update_call(where, all1, f1, wt, None, (0, 2), [g2])
    (all2,) = spread(where, g2, [loss1])
    w1, _ = update_call(where, all1, f1, wt, w1, (1, 2), [all2[2]])
    w2, losses = update_call(where, all2, f2, w1, w1, loss=loss1)
    return w2.T, losses.reshape(2)


def plain_device(nfeat, ncls, inputs, projection, offsets, labels, weights):
    phase = offsets.astype(f32) * (2.0 * math.pi / 65521.0) - math.pi
    classes = jnp.arange(weights.shape[1], dtype=jnp.int32) + lax.axis_index("cls") * weights.shape[1]
    losses = []
    for p in range(inputs.shape[0]):
        x = lax.all_gather(inputs[p], "feat", axis=0, tiled=True)
        features = (math.sqrt(2.0 / nfeat) * jnp.cos(jnp.dot(x, projection, preferred_element_type=f32) + phase)).astype(bf16)
        scores = lax.psum(jnp.dot(features, weights.astype(bf16), preferred_element_type=f32), "feat")
        is_target = labels[p][:, None] == classes[None, :]
        target = lax.psum(jnp.sum(jnp.where(is_target, scores, 0.0), axis=1), "cls")
        margin = jnp.where(is_target, 0.0, jnp.maximum(0.0, 1.0 + scores - target[:, None]))
        slope = 2.0 * margin / (ncls - 1)
        others, row_loss = lax.psum((jnp.sum(slope, axis=1), jnp.sum(margin * margin, axis=1) / (ncls - 1)), "cls")
        grad = jnp.where(is_target, -others[:, None], slope).astype(bf16)
        weights = weights - learning_rate * lax.dot_general(features, grad, (((0,), (0,)), ((), ())), preferred_element_type=f32)
        losses.append(jnp.sum(row_loss))
    return weights, jnp.stack(losses)


def solution(mesh):
    kernels = mesh.shape["feat"] == 8 and mesh.shape["cls"] == 4

    def program(inputs, projection, offsets, labels, weights):
        nfeat, ncls = weights.shape
        body = per_device if kernels and inputs.shape[:2] == (2, 1024) else plain_device
        return jax.shard_map(
            functools.partial(body, nfeat, ncls),
            mesh=mesh,
            in_specs=(P(None, "feat", None), P(None, "feat"), P("feat"), P(), P("feat", "cls")),
            out_specs=(P("feat", "cls"), P()),
            check_vma=False,
        )(inputs, projection, offsets, labels, weights)

    return program
```

profile of v0, /device:TPU:0, one launch (start us, length us, event | category | flops | bytes accessed | tf_op | source)
XLA Modules:
  0.0 334.2 jit_solution(13420144416789841907)
XLA Ops:
  0.6 1.0 slice_bitcast_fusion
  1.6 5.1 %collective-permute-start = (bf16[360,128]{1,0:T(8,128)(2,1)S(1)}, bf16[360,128]{1,0:T(8,128)(2,1)S(1)}, u32[]{:S(2)}, u32[]{:S(2)}) collective-permute-start(bf16[360,128]{1,0:T(8,128)(2,1)S(1)} %get-tuple-element.79.refs_1_), channel_id=1, source_target_pairs={{0,24},{4,28},{8,16},{12,20},{16,8},{20,12},{24,0},{28,4},{1,25},{... | collective-permute-start | bytes 276488 | tf_op jit(solution)/shard_map/ppermute | solution.py:194
  6.7 1.2 collective-permute-start.1
  7.9 0.8 collective-permute-start.2
  8.7 1.9 collective-permute-start.3
  10.6 1.4 collective-permute-start.4
  12.1 6.3 %collective-permute-start.5 = (bf16[360,128]{1,0:T(8,128)(2,1)S(1)}, bf16[360,128]{1,0:T(8,128)(2,1)S(1)}, u32[]{:S(2)}, u32[]{:S(2)}) collective-permute-start(bf16[360,128]{1,0:T(8,128)(2,1)S(1)} %get-tuple-element.79.refs_1_), channel_id=1, source_target_pairs={{0,12},{4,8},{8,4},{12,0},{16,28},{20,24},{24,20},{28,16},{1,13},{... | collective-permute-start | bytes 276488 | tf_op jit(solution)/shard_map/ppermute | solution.py:194
  18.7 2.8 collective-permute-done.2.refs_3_
  21.4 1.5 collective-permute-start.8
  23.0 0.5 collective-permute-done.3.refs_4_
  23.5 0.7 collective-permute-done.5.refs_6_
  24.2 1.5 collective-permute-done.6.refs_11_
  25.7 2.7 copy-done.2
  28.4 0.8 copy-done.11
  29.2 37.1 %features_scores.4 = (bf16[1024,8192]{1,0:T(8,128)(2,1)}, bf16[3,1264,128]{2,1,0:T(8,128)(2,1)S(1)}, f32[3,1264,128]{2,1,0:T(8,128)S(1)}, bf16[1264,8192]{1,0:T(8,128)(2,1)}, bf16[2,360,128]{2,1,0:T(8,128)(2,1)S(1)}) custom-call(s32[4]{0:T(128)S(1)} %pad_add_fusion.refs_0_.where_ref, bf16[360,128]{1,0:T(8,128)(2,1)S(1)} %collective-permute-done.refs_1_, ...), custom_call_target="tpu_custom_call" | custom-call | flops 20434649088 | bytes 33292288 | tf_op jit(solution)/shard_map/features_scores/pallas_call | solution.py:137
  66.3 1.5 collective-permute-start.10
  67.8 2.7 collective-permute-start.7
  70.7 16.7 %features_scores.5 = (bf16[1024,8192]{1,0:T(8,128)(2,1)}, bf16[1,1264,128]{2,1,0:T(8,128)(2,1)S(1)}, f32[1,1264,128]{2,1,0:T(8,128)S(1)}) custom-call(s32[4]{0:T(128)S(1)} %pad_add_fusion.refs_0_.where_ref, bf16[360,128]{1,0:T(8,128)(2,1)S(1)} %get-tuple-element.79.refs_1_, ...), custom_call_target="tpu_custom_call", output_to_operand_aliasing={{0}: (6, {})} | custom-call | flops 6811549696 | bytes 24903680 | tf_op jit(solution)/shard_map/features_scores/pallas_call | solution.py:137
  87.5 0.8 pair_sums.3
  88.3 2.1 collective-permute-start.12
  90.3 2.7 collective-permute-start.13
  93.0 1.7 collective-permute-start.15
  94.7 27.2 %features_scores.6 = (bf16[1024,8192]{1,0:T(8,128)(2,1)}, bf16[2,1520,128]{2,1,0:T(8,128)(2,1)S(1)}, f32[2,1520,128]{2,1,0:T(8,128)S(1)}) custom-call(s32[4]{0:T(128)S(1)} %pad_add_fusion.refs_0_.where_ref, bf16[2,360,128]{2,1,0:T(8,128)(2,1)S(1)} %collective-permute-done.9.refs_4_.refs_1_, bf16[2,360,128]{2,1,0:T(8,128)(2,1)S(1)} %collective-permute-done.10.refs_5_.refs_2_, ...), custom_call_target="tpu_custom_call" | custom-call | flops 15770583040 | bytes 29097984 | tf_op jit(solution)/shard_map/features_scores/pallas_call | solution.py:137
  122.0 1.1 target.2
  123.1 0.8 copy-done.5
  124.0 5.6 %psum.28.refs_3_ = f32[1,128]{1,0:T(1,128)S(1)} all-reduce(f32[1,128]{1,0:T(1,128)S(1)} %get-tuple-element.57), channel_id=1, replica_groups=mesh['feat'=8,'cls'=4] {'cls'}, use_global_device_ids=true, to_apply=%region_0.0 | all-reduce | flops 128 | bytes 1024 | tf_op jit(solution)/shard_map/psum | solution.py:378
  129.6 1.1 copy-done.6
  130.7 0.8 margin.2
  131.5 0.8 copy-done.7
  132.3 7.0 %psum.29.refs_3_ = f32[2,128]{1,0:T(2,128)S(1)} all-reduce(f32[2,128]{1,0:T(2,128)S(1)} %get-tuple-element.59), channel_id=1, replica_groups=mesh['feat'=8,'cls'=4] {'cls'}, use_global_device_ids=true, to_apply=%region_1.0 | all-reduce | flops 256 | bytes 2048 | tf_op jit(solution)/shard_map/psum | solution.py:385
  139.3 1.1 copy-done.8
  140.4 0.6 step_grad.2.refs_3_.refs_10_.refs_0_
  141.0 1.3 collective-permute-start.17
  142.3 2.5 collective-permute-start.18
  144.9 0.6 collective-permute-start.19
  145.5 1.8 pair_sums.4
  147.3 2.7 copy-done.4
  150.0 27.0 %features_scores.7 = (bf16[1024,8192]{1,0:T(8,128)(2,1)}, bf16[2,1520,128]{2,1,0:T(8,128)(2,1)S(1)}, f32[2,1520,128]{2,1,0:T(8,128)S(1)}) custom-call(s32[4]{0:T(128)S(1)} %pad_add_fusion.refs_0_.where_ref, bf16[2,360,128]{2,1,0:T(8,128)(2,1)S(1)} %collective-permute-done.7.refs_6_.refs_1_, ...), custom_call_target="tpu_custom_call", output_to_operand_aliasing={{0}: (7, {})} | custom-call | flops 15770583040 | bytes 29097984 | tf_op jit(solution)/shard_map/features_scores/pallas_call | solution.py:137
  177.0 0.6 line.2
  177.7 1.6 collective-permute-start.20
  179.7 1.0 collective-permute-start.22
  180.8 2.2 collective-permute-start.23
  182.9 15.1 %collective-permute-done.20.refs_2_ = bf16[2,1520,128]{2,1,0:T(8,128)(2,1)S(1)} collective-permute-done((bf16[2,1520,128]{2,1,0:T(8,128)(2,1)S(1)}, bf16[2,1520,128]{2,1,0:T(8,128)(2,1)S(1)}, u32[]{:S(2)}, u32[]{:S(2)}) %collective-permute-start.20) | collective-permute-done | bytes 778272 | tf_op jit(solution)/shard_map/ppermute | solution.py:194
  198.0 0.7 pair_sums.5
  199.1 1.3 collective-permute-start.27
  200.4 6.5 %collective-permute-done.22.refs_3_ = bf16[1520,128]{1,0:T(8,128)(2,1)S(1)} collective-permute-done((bf16[1520,128]{1,0:T(8,128)(2,1)S(1)}, bf16[1520,128]{1,0:T(8,128)(2,1)S(1)}, u32[]{:S(2)}, u32[]{:S(2)}) %collective-permute-start.22) | collective-permute-done | bytes 389152 | tf_op jit(solution)/shard_map/ppermute | solution.py:194
  206.9 7.5 %collective-permute-done.21.refs_2_ = bf16[1520,128]{1,0:T(8,128)(2,1)S(1)} collective-permute-done((bf16[1520,128]{1,0:T(8,128)(2,1)S(1)}, bf16[1520,128]{1,0:T(8,128)(2,1)S(1)}, u32[]{:S(2)}, u32[]{:S(2)}) %collective-permute-start.21) | collective-permute-done | bytes 389152 | tf_op jit(solution)/shard_map/ppermute | solution.py:194
  214.4 0.6 gram.1.refs_6_
  215.0 1.6 collective-permute-start.25
  216.9 6.1 %collective-permute-done.27.refs_11_.refs_1_ = bf16[1264,128]{1,0:T(8,128)(2,1)S(1)} collective-permute-done((bf16[1264,128]{1,0:T(8,128)(2,1)S(1)}, bf16[1264,128]{1,0:T(8,128)(2,1)S(1)}, u32[]{:S(2)}, u32[]{:S(2)}) %collective-permute-start.27) | collective-permute-done | bytes 323616 | tf_op jit(solution)/shard_map/ppermute | solution.py:194
  223.0 2.1 target.3
  225.1 5.7 %psum.30.refs_3_ = f32[1,128]{1,0:T(1,128)S(1)} all-reduce(f32[1,128]{1,0:T(1,128)S(1)} %get-tuple-element.69), channel_id=1, replica_groups=mesh['feat'=8,'cls'=4] {'cls'}, use_global_device_ids=true, to_apply=%region_2.0 | all-reduce | flops 128 | bytes 1024 | tf_op jit(solution)/shard_map/psum | solution.py:378
  230.8 0.8 margin.3
  231.6 0.8 copy-done.9
  232.4 6.6 %psum.31.refs_3_ = f32[2,128]{1,0:T(2,128)S(1)} all-reduce(f32[2,128]{1,0:T(2,128)S(1)} %get-tuple-element.71), channel_id=1, replica_groups=mesh['feat'=8,'cls'=4] {'cls'}, use_global_device_ids=true, to_apply=%region_3.0 | all-reduce | flops 256 | bytes 2048 | tf_op jit(solution)/shard_map/psum | solution.py:385
  239.0 1.1 copy-done.10
  240.1 0.6 step_grad.3.refs_6_.refs_0_
  240.7 0.5 collective-permute-start.30
  241.2 3.5 %collective-permute-start.31 = (bf16[1264,128]{1,0:T(8,128)(2,1)S(1)}, bf16[1264,128]{1,0:T(8,128)(2,1)S(1)}, u32[]{:S(2)}, u32[]{:S(2)}) collective-permute-start(bf16[1264,128]{1,0:T(8,128)(2,1)S(1)} %step_grad.3.refs_6_.refs_0_), channel_id=1, source_target_pairs={{0,16},{4,20},{8,24},{12,28},{16,0},{20,4},{24,8},{28,12},{1,17},{... | collective-permute-start | bytes 970760 | tf_op jit(solution)/shard_map/ppermute | solution.py:194
  245.2 1.7 collective-permute-start.29
  246.9 22.3 %update.3 = (f32[1250,8192]{1,0:T(8,128)}, f32[1,2]{1,0:T(1,128)S(1)}) custom-call(s32[4]{0:T(128)S(1)} %pad_add_fusion.refs_0_.where_ref, bf16[1264,128]{1,0:T(8,128)(2,1)S(1)} %step_grad.2.refs_3_.refs_10_.refs_0_, bf16[1264,128]{1,0:T(8,128)(2,1)S(1)} %collective-permute-done.27.refs_11_.refs_1_, ...), custom_call_target="tpu_custom_call" | custom-call | flops 10603200512 | bytes 49807360 | tf_op jit(solution)/shard_map/update/pallas_call | solution.py:327
  269.2 0.6 line.3.refs_7_.refs_2_
  270.2 22.3 %update.4 = (f32[1250,8192]{1,0:T(8,128)}, f32[1,2]{1,0:T(1,128)}) custom-call(s32[4]{0:T(128)S(1)} %pad_add_fusion.refs_0_.where_ref, bf16[1264,128]{1,0:T(8,128)(2,1)S(1)} %step_grad.2.refs_3_.refs_10_.refs_0_, bf16[1264,128]{1,0:T(8,128)(2,1)S(1)} %collective-permute-done.27.refs_11_.refs_1_, ...), custom_call_target="tpu_custom_call", output_to_operand_aliasing={{0}: (7, {})} | custom-call | flops 10603200512 | bytes 49807360 | tf_op jit(solution)/shard_map/update/pallas_call | solution.py:327
  292.5 41.7 %update.5 = (f32[1250,8192]{1,0:T(8,128)}, f32[1,2]{1,0:T(1,128)}) custom-call(s32[4]{0:T(128)S(1)} %pad_add_fusion.refs_0_.where_ref, bf16[1264,128]{1,0:T(8,128)(2,1)S(1)} %step_grad.3.refs_6_.refs_0_, bf16[1264,128]{1,0:T(8,128)(2,1)S(1)} %collective-permute-done.29.refs_1_, ...), custom_call_target="tpu_custom_call", output_to_operand_aliasing={{0}: (6, {})} | custom-call | flops 21206401024 | bytes 99614720 | tf_op jit(solution)/shard_map/update/pallas_call | solution.py:327
  (57 shorter events, 2.7 us)
Async XLA Ops:
  0.6 65.6 %copy-start = (s32[2,1024]{1,0:T(2,128)S(1)}, s32[2,1024]{1,0:T(2,128)}, u32[]{:S(2)}) copy-start(s32[2,1024]{1,0:T(2,128)} %param.8) | copy-start | bytes 24580
  1.6 10.5 %collective-permute-start = (bf16[360,128]{1,0:T(8,128)(2,1)S(1)}, bf16[360,128]{1,0:T(8,128)(2,1)S(1)}, u32[]{:S(2)}, u32[]{:S(2)}) collective-permute-start(bf16[360,128]{1,0:T(8,128)(2,1)S(1)} %get-tuple-element.79.refs_1_), channel_id=1, source_target_pairs={{0,24},{4,28},{8,16},{12,20},{16,8},{20,12},{24,0},{28,4},{1,25},{... | collective-permute-start | bytes 276488 | tf_op jit(solution)/shard_map/ppermute | solution.py:194
  6.7 11.6 %collective-permute-start.1 = (bf16[360,128]{1,0:T(8,128)(2,1)S(1)}, bf16[360,128]{1,0:T(8,128)(2,1)S(1)}, u32[]{:S(2)}, u32[]{:S(2)}) collective-permute-start(bf16[360,128]{1,0:T(8,128)(2,1)S(1)} %get-tuple-element.79.refs_1_), channel_id=1, source_target_pairs={{0,28},{4,24},{8,20},{12,16},{16,12},{20,8},{24,4},{28,0},{1,29},{... | collective-permute-start | bytes 276488 | tf_op jit(solution)/shard_map/ppermute | solution.py:194
  7.9 13.5 %collective-permute-start.2 = (bf16[360,128]{1,0:T(8,128)(2,1)S(1)}, bf16[360,128]{1,0:T(8,128)(2,1)S(1)}, u32[]{:S(2)}, u32[]{:S(2)}) collective-permute-start(bf16[360,128]{1,0:T(8,128)(2,1)S(1)} %get-tuple-element.79.refs_1_), channel_id=1, source_target_pairs={{0,16},{4,20},{8,24},{12,28},{16,0},{20,4},{24,8},{28,12},{1,17},{... | collective-permute-start | bytes 276488 | tf_op jit(solution)/shard_map/ppermute | solution.py:194
  8.7 14.8 %collective-permute-start.3 = (bf16[360,128]{1,0:T(8,128)(2,1)S(1)}, bf16[360,128]{1,0:T(8,128)(2,1)S(1)}, u32[]{:S(2)}, u32[]{:S(2)}) collective-permute-start(bf16[360,128]{1,0:T(8,128)(2,1)S(1)} %get-tuple-element.79.refs_1_), channel_id=1, source_target_pairs={{0,20},{4,16},{8,28},{12,24},{16,4},{20,0},{24,12},{28,8},{1,21},{... | collective-permute-start | bytes 276488 | tf_op jit(solution)/shard_map/ppermute | solution.py:194
  10.6 12.9 %collective-permute-start.4 = (bf16[360,128]{1,0:T(8,128)(2,1)S(1)}, bf16[360,128]{1,0:T(8,128)(2,1)S(1)}, u32[]{:S(2)}, u32[]{:S(2)}) collective-permute-start(bf16[360,128]{1,0:T(8,128)(2,1)S(1)} %get-tuple-element.79.refs_1_), channel_id=1, source_target_pairs={{0,8},{4,12},{8,0},{12,4},{16,24},{20,28},{24,16},{28,20},{1,9},{5... | collective-permute-start | bytes 276488 | tf_op jit(solution)/shard_map/ppermute | solution.py:194
  12.1 12.1 %collective-permute-start.5 = (bf16[360,128]{1,0:T(8,128)(2,1)S(1)}, bf16[360,128]{1,0:T(8,128)(2,1)S(1)}, u32[]{:S(2)}, u32[]{:S(2)}) collective-permute-start(bf16[360,128]{1,0:T(8,128)(2,1)S(1)} %get-tuple-element.79.refs_1_), channel_id=1, source_target_pairs={{0,12},{4,8},{8,4},{12,0},{16,28},{20,24},{24,20},{28,16},{1,13},{... | collective-permute-start | bytes 276488 | tf_op jit(solution)/shard_map/ppermute | solution.py:194
  18.4 7.4 %collective-permute-start.6 = (bf16[360,128]{1,0:T(8,128)(2,1)S(1)}, bf16[360,128]{1,0:T(8,128)(2,1)S(1)}, u32[]{:S(2)}, u32[]{:S(2)}) collective-permute-start(bf16[360,128]{1,0:T(8,128)(2,1)S(1)} %get-tuple-element.78.refs_10_), channel_id=1, source_target_pairs={{0,4},{4,0},{8,12},{12,8},{16,20},{20,16},{24,28},{28,24},{1,5},{5... | collective-permute-start | bytes 276488 | tf_op jit(solution)/shard_map/ppermute | solution.py:194
  21.4 49.3 %collective-permute-start.8 = (bf16[360,128]{1,0:T(8,128)(2,1)S(1)}, bf16[360,128]{1,0:T(8,128)(2,1)S(1)}, u32[]{:S(2)}, u32[]{:S(2)}) collective-permute-start(bf16[360,128]{1,0:T(8,128)(2,1)S(1)} %get-tuple-element.79.refs_1_), channel_id=1, source_target_pairs={{0,4},{4,0},{8,12},{12,8},{16,20},{20,16},{24,28},{28,24},{1,5},{5... | collective-permute-start | bytes 276488 | tf_op jit(solution)/shard_map/ppermute | solution.py:194
  25.7 2.7 copy-start.2
  28.4 0.8 copy-start.11
  29.2 41.6 %copy-start.3 = (bf16[360,8192]{1,0:T(8,128)(2,1)S(1)}, bf16[360,8192]{1,0:T(8,128)(2,1)}, u32[]{:S(2)}) copy-start(bf16[360,8192]{1,0:T(8,128)(2,1)} %refs_3_.5) | copy-start | bytes 17694724
  66.2 21.2 %collective-permute-start.11 = (bf16[3,1264,128]{2,1,0:T(8,128)(2,1)S(1)}, bf16[3,1264,128]{2,1,0:T(8,128)(2,1)S(1)}, u32[]{:S(2)}, u32[]{:S(2)}) collective-permute-start(bf16[3,1264,128]{2,1,0:T(8,128)(2,1)S(1)} %get-tuple-element.45), channel_id=1, source_target_pairs={{0,4},{4,0},{8,12},{12,8},{16,20},{20,16},{24,28},{28,24},{1,5},{5... | collective-permute-start | bytes 2912264 | tf_op jit(solution)/shard_map/ppermute | solution.py:194
  66.3 21.2 %collective-permute-start.10 = (bf16[2,360,128]{2,1,0:T(8,128)(2,1)S(1)}, bf16[2,360,128]{2,1,0:T(8,128)(2,1)S(1)}, u32[]{:S(2)}, u32[]{:S(2)}) collective-permute-start(bf16[2,360,128]{2,1,0:T(8,128)(2,1)S(1)} %get-tuple-element.40.refs_7_.refs_2_), channel_id=1, source_target_pairs={{0,16},{4,20},{8,24},{12,28},{16,0},{20,4},{24,8},{28,12},{1,17},{... | collective-permute-start | bytes 552968 | tf_op jit(solution)/shard_map/ppermute | solution.py:194
  67.8 19.6 %collective-permute-start.7 = (bf16[2,360,128]{2,1,0:T(8,128)(2,1)S(1)}, bf16[2,360,128]{2,1,0:T(8,128)(2,1)S(1)}, u32[]{:S(2)}, u32[]{:S(2)}) collective-permute-start(bf16[2,360,128]{2,1,0:T(8,128)(2,1)S(1)} %get-tuple-element.40.refs_7_.refs_2_), channel_id=1, source_target_pairs={{0,8},{4,12},{8,0},{12,4},{16,24},{20,28},{24,16},{28,20},{1,9},{5... | collective-permute-start | bytes 552968 | tf_op jit(solution)/shard_map/ppermute | solution.py:194
  70.5 16.9 %collective-permute-start.9 = (bf16[2,360,128]{2,1,0:T(8,128)(2,1)S(1)}, bf16[2,360,128]{2,1,0:T(8,128)(2,1)S(1)}, u32[]{:S(2)}, u32[]{:S(2)}) collective-permute-start(bf16[2,360,128]{2,1,0:T(8,128)(2,1)S(1)} %get-tuple-element.40.refs_7_.refs_2_), channel_id=1, source_target_pairs={{0,24},{4,28},{8,16},{12,20},{16,8},{20,12},{24,0},{28,4},{1,25},{... | collective-permute-start | bytes 552968 | tf_op jit(solution)/shard_map/ppermute | solution.py:194
  70.7 24.0 %copy-start.12 = (s32[8192]{0:T(1024)S(1)}, s32[8192]{0:T(1024)}, u32[]{:S(2)}) copy-start(s32[8192]{0:T(1024)} %param.7) | copy-start | bytes 98308
  88.3 33.7 %collective-permute-start.12 = (bf16[1,1264,128]{2,1,0:T(8,128)(2,1)S(1)}, bf16[1,1264,128]{2,1,0:T(8,128)(2,1)S(1)}, u32[]{:S(2)}, u32[]{:S(2)}) collective-permute-start(bf16[1,1264,128]{2,1,0:T(8,128)(2,1)S(1)} %get-tuple-element.51), channel_id=1, source_target_pairs={{0,4},{4,0},{8,12},{12,8},{16,20},{20,16},{24,28},{28,24},{1,5},{5... | collective-permute-start | bytes 970760 | tf_op jit(solution)/shard_map/ppermute | solution.py:194
  90.3 31.6 %collective-permute-start.13 = (bf16[1264,128]{1,0:T(8,128)(2,1)S(1)}, bf16[1264,128]{1,0:T(8,128)(2,1)S(1)}, u32[]{:S(2)}, u32[]{:S(2)}) collective-permute-start(bf16[1264,128]{1,0:T(8,128)(2,1)S(1)} %get-tuple-element.48.refs_7_), channel_id=1, source_target_pairs={{0,24},{4,28},{8,16},{12,20},{16,8},{20,12},{24,0},{28,4},{1,25},{... | collective-permute-start | bytes 970760 | tf_op jit(solution)/shard_map/ppermute | solution.py:194
  93.0 28.9 %collective-permute-start.14 = (bf16[1264,128]{1,0:T(8,128)(2,1)S(1)}, bf16[1264,128]{1,0:T(8,128)(2,1)S(1)}, u32[]{:S(2)}, u32[]{:S(2)}) collective-permute-start(bf16[1264,128]{1,0:T(8,128)(2,1)S(1)} %get-tuple-element.52), channel_id=1, source_target_pairs={{0,16},{4,20},{8,24},{12,28},{16,0},{20,4},{24,8},{28,12},{1,17},{... | collective-permute-start | bytes 970760 | tf_op jit(solution)/shard_map/ppermute | solution.py:194
  93.0 28.9 %collective-permute-start.15 = (bf16[1264,128]{1,0:T(8,128)(2,1)S(1)}, bf16[1264,128]{1,0:T(8,128)(2,1)S(1)}, u32[]{:S(2)}, u32[]{:S(2)}) collective-permute-start(bf16[1264,128]{1,0:T(8,128)(2,1)S(1)} %get-tuple-element.53), channel_id=1, source_target_pairs={{0,8},{4,12},{8,0},{12,4},{16,24},{20,28},{24,16},{28,20},{1,9},{5... | collective-permute-start | bytes 970760 | tf_op jit(solution)/shard_map/ppermute | solution.py:194
  123.1 0.8 copy-start.5
  123.9 21.6 %collective-permute-start.16 = (bf16[2,1520,128]{2,1,0:T(8,128)(2,1)S(1)}, bf16[2,1520,128]{2,1,0:T(8,128)(2,1)}, u32[]{:S(2)}, u32[]{:S(2)}) collective-permute-start(bf16[2,1520,128]{2,1,0:T(8,128)(2,1)S(1)} %get-tuple-element.55), channel_id=1, source_target_pairs={{0,4},{4,0},{8,12},{12,8},{16,20},{20,16},{24,28},{28,24},{1,5},{5... | collective-permute-start | bytes 2334728 | tf_op jit(solution)/shard_map/ppermute | solution.py:194
  129.6 1.1 copy-start.6
  131.5 0.8 copy-start.7
  139.3 1.1 copy-start.8
  141.0 36.0 %collective-permute-start.17 = (bf16[1264,128]{1,0:T(8,128)(2,1)S(1)}, bf16[1264,128]{1,0:T(8,128)(2,1)S(1)}, u32[]{:S(2)}, u32[]{:S(2)}) collective-permute-start(bf16[1264,128]{1,0:T(8,128)(2,1)S(1)} %step_grad.2.refs_3_.refs_10_.refs_0_), channel_id=1, source_target_pairs={{0,8},{4,12},{8,0},{12,4},{16,24},{20,28},{24,16},{28,20},{1,9},{5... | collective-permute-start | bytes 970760 | tf_op jit(solution)/shard_map/ppermute | solution.py:194
  142.3 34.7 %collective-permute-start.18 = (bf16[1264,128]{1,0:T(8,128)(2,1)S(1)}, bf16[1264,128]{1,0:T(8,128)(2,1)S(1)}, u32[]{:S(2)}, u32[]{:S(2)}) collective-permute-start(bf16[1264,128]{1,0:T(8,128)(2,1)S(1)} %step_grad.2.refs_3_.refs_10_.refs_0_), channel_id=1, source_target_pairs={{0,16},{4,20},{8,24},{12,28},{16,0},{20,4},{24,8},{28,12},{1,17},{... | collective-permute-start | bytes 970760 | tf_op jit(solution)/shard_map/ppermute | solution.py:194
  144.9 32.2 %collective-permute-start.19 = (bf16[1264,128]{1,0:T(8,128)(2,1)S(1)}, bf16[1264,128]{1,0:T(8,128)(2,1)S(1)}, u32[]{:S(2)}, u32[]{:S(2)}) collective-permute-start(bf16[1264,128]{1,0:T(8,128)(2,1)S(1)} %step_grad.2.refs_3_.refs_10_.refs_0_), channel_id=1, source_target_pairs={{0,24},{4,28},{8,16},{12,20},{16,8},{20,12},{24,0},{28,4},{1,25},{... | collective-permute-start | bytes 970760 | tf_op jit(solution)/shard_map/ppermute | solution.py:194
  147.3 2.7 copy-start.4
  177.7 20.4 %collective-permute-start.20 = (bf16[2,1520,128]{2,1,0:T(8,128)(2,1)S(1)}, bf16[2,1520,128]{2,1,0:T(8,128)(2,1)S(1)}, u32[]{:S(2)}, u32[]{:S(2)}) collective-permute-start(bf16[2,1520,128]{2,1,0:T(8,128)(2,1)S(1)} %get-tuple-element.63), channel_id=1, source_target_pairs={{0,4},{4,0},{8,12},{12,8},{16,20},{20,16},{24,28},{28,24},{1,5},{5... | collective-permute-start | bytes 2334728 | tf_op jit(solution)/shard_map/ppermute | solution.py:194
  179.3 43.7 %collective-permute-start.28 = (bf16[3,1264,128]{2,1,0:T(8,128)(2,1)S(1)}, bf16[3,1264,128]{2,1,0:T(8,128)(2,1)S(1)}, u32[]{:S(2)}, u32[]{:S(2)}) collective-permute-start(bf16[3,1264,128]{2,1,0:T(8,128)(2,1)S(1)} %get-tuple-element.64.refs_3_.refs_12_.refs_2_), channel_id=1, source_target_pairs={{0,4},{4,0},{8,12},{12,8},{16,20},{20,16},{24,28},{28,24},{1,5},{5... | collective-permute-start | bytes 2912264 | tf_op jit(solution)/shard_map/ppermute | solution.py:194
  179.7 27.2 %collective-permute-start.22 = (bf16[1520,128]{1,0:T(8,128)(2,1)S(1)}, bf16[1520,128]{1,0:T(8,128)(2,1)S(1)}, u32[]{:S(2)}, u32[]{:S(2)}) collective-permute-start(bf16[1520,128]{1,0:T(8,128)(2,1)S(1)} %get-tuple-element.60.refs_8_), channel_id=1, source_target_pairs={{0,16},{4,20},{8,24},{12,28},{16,0},{20,4},{24,8},{28,12},{1,17},{... | collective-permute-start | bytes 1167368 | tf_op jit(solution)/shard_map/ppermute | solution.py:194
  180.8 26.1 %collective-permute-start.23 = (bf16[1520,128]{1,0:T(8,128)(2,1)S(1)}, bf16[1520,128]{1,0:T(8,128)(2,1)S(1)}, u32[]{:S(2)}, u32[]{:S(2)}) collective-permute-start(bf16[1520,128]{1,0:T(8,128)(2,1)S(1)} %get-tuple-element.67), channel_id=1, source_target_pairs={{0,24},{4,28},{8,16},{12,20},{16,8},{20,12},{24,0},{28,4},{1,25},{... | collective-permute-start | bytes 1167368 | tf_op jit(solution)/shard_map/ppermute | solution.py:194
  198.7 15.6 %collective-permute-start.21 = (bf16[1520,128]{1,0:T(8,128)(2,1)S(1)}, bf16[1520,128]{1,0:T(8,128)(2,1)S(1)}, u32[]{:S(2)}, u32[]{:S(2)}) collective-permute-start(bf16[1520,128]{1,0:T(8,128)(2,1)S(1)} %get-tuple-element.66), channel_id=1, source_target_pairs={{0,8},{4,12},{8,0},{12,4},{16,24},{20,28},{24,16},{28,20},{1,9},{5... | collective-permute-start | bytes 1167368 | tf_op jit(solution)/shard_map/ppermute | solution.py:194
  199.1 23.9 %collective-permute-start.27 = (bf16[1264,128]{1,0:T(8,128)(2,1)S(1)}, bf16[1264,128]{1,0:T(8,128)(2,1)S(1)}, u32[]{:S(2)}, u32[]{:S(2)}) collective-permute-start(bf16[1264,128]{1,0:T(8,128)(2,1)S(1)} %step_grad.2.refs_3_.refs_10_.refs_0_), channel_id=1, source_target_pairs={{0,4},{4,0},{8,12},{12,8},{16,20},{20,16},{24,28},{28,24},{1,5},{5... | collective-permute-start | bytes 970760 | tf_op jit(solution)/shard_map/ppermute | solution.py:194
  215.0 8.0 %collective-permute-start.24 = (bf16[256,128]{1,0:T(8,128)(2,1)S(1)}, bf16[256,128]{1,0:T(8,128)(2,1)S(1)}, u32[]{:S(2)}, u32[]{:S(2)}) collective-permute-start(bf16[256,128]{1,0:T(8,128)(2,1)S(1)} %gram.1.refs_6_), channel_id=1, source_target_pairs={{0,1},{1,0},{2,3},{3,2},{4,5},{5,4},{6,7},{7,6},{8,9},{9,8},{10,11... | collective-permute-start | bytes 196616 | tf_op jit(solution)/shard_map/ppermute | solution.py:203
  215.0 8.0 %collective-permute-start.25 = (bf16[256,128]{1,0:T(8,128)(2,1)S(1)}, bf16[256,128]{1,0:T(8,128)(2,1)S(1)}, u32[]{:S(2)}, u32[]{:S(2)}) collective-permute-start(bf16[256,128]{1,0:T(8,128)(2,1)S(1)} %gram.1.refs_6_), channel_id=1, source_target_pairs={{0,2},{1,3},{2,0},{3,1},{4,6},{5,7},{6,4},{7,5},{8,10},{9,11},{10,... | collective-permute-start | bytes 196616 | tf_op jit(solution)/shard_map/ppermute | solution.py:203
  216.6 6.4 %collective-permute-start.26 = (bf16[256,128]{1,0:T(8,128)(2,1)S(1)}, bf16[256,128]{1,0:T(8,128)(2,1)S(1)}, u32[]{:S(2)}, u32[]{:S(2)}) collective-permute-start(bf16[256,128]{1,0:T(8,128)(2,1)S(1)} %gram.1.refs_6_), channel_id=1, source_target_pairs={{0,3},{1,2},{2,1},{3,0},{4,7},{5,6},{6,5},{7,4},{8,11},{9,10},{10,... | collective-permute-start | bytes 196616 | tf_op jit(solution)/shard_map/ppermute | solution.py:203
  231.6 0.8 copy-start.9
  239.0 1.1 copy-start.10
  240.7 28.5 %collective-permute-start.30 = (bf16[1264,128]{1,0:T(8,128)(2,1)S(1)}, bf16[1264,128]{1,0:T(8,128)(2,1)S(1)}, u32[]{:S(2)}, u32[]{:S(2)}) collective-permute-start(bf16[1264,128]{1,0:T(8,128)(2,1)S(1)} %step_grad.3.refs_6_.refs_0_), channel_id=1, source_target_pairs={{0,8},{4,12},{8,0},{12,4},{16,24},{20,28},{24,16},{28,20},{1,9},{5... | collective-permute-start | bytes 970760 | tf_op jit(solution)/shard_map/ppermute | solution.py:194
  241.2 28.0 %collective-permute-start.31 = (bf16[1264,128]{1,0:T(8,128)(2,1)S(1)}, bf16[1264,128]{1,0:T(8,128)(2,1)S(1)}, u32[]{:S(2)}, u32[]{:S(2)}) collective-permute-start(bf16[1264,128]{1,0:T(8,128)(2,1)S(1)} %step_grad.3.refs_6_.refs_0_), channel_id=1, source_target_pairs={{0,16},{4,20},{8,24},{12,28},{16,0},{20,4},{24,8},{28,12},{1,17},{... | collective-permute-start | bytes 970760 | tf_op jit(solution)/shard_map/ppermute | solution.py:194
  244.8 24.5 %collective-permute-start.32 = (bf16[1264,128]{1,0:T(8,128)(2,1)S(1)}, bf16[1264,128]{1,0:T(8,128)(2,1)S(1)}, u32[]{:S(2)}, u32[]{:S(2)}) collective-permute-start(bf16[1264,128]{1,0:T(8,128)(2,1)S(1)} %step_grad.3.refs_6_.refs_0_), channel_id=1, source_target_pairs={{0,24},{4,28},{8,16},{12,20},{16,8},{20,12},{24,0},{28,4},{1,25},{... | collective-permute-start | bytes 970760 | tf_op jit(solution)/shard_map/ppermute | solution.py:194
  245.2 47.3 %collective-permute-start.29 = (bf16[1264,128]{1,0:T(8,128)(2,1)S(1)}, bf16[1264,128]{1,0:T(8,128)(2,1)S(1)}, u32[]{:S(2)}, u32[]{:S(2)}) collective-permute-start(bf16[1264,128]{1,0:T(8,128)(2,1)S(1)} %step_grad.3.refs_6_.refs_0_), channel_id=1, source_target_pairs={{0,4},{4,0},{8,12},{12,8},{16,20},{20,16},{24,28},{28,24},{1,5},{5... | collective-permute-start | bytes 970760 | tf_op jit(solution)/shard_map/ppermute | solution.py:194
  269.8 22.6 %collective-permute-start.33 = (bf16[3,1264,128]{2,1,0:T(8,128)(2,1)S(1)}, bf16[3,1264,128]{2,1,0:T(8,128)(2,1)S(1)}, u32[]{:S(2)}, u32[]{:S(2)}) collective-permute-start(bf16[3,1264,128]{2,1,0:T(8,128)(2,1)S(1)} %line.3.refs_7_.refs_2_), channel_id=1, source_target_pairs={{0,4},{4,0},{8,12},{12,8},{16,20},{20,16},{24,28},{28,24},{1,5},{5... | collective-permute-start | bytes 2912264 | tf_op jit(solution)/shard_map/ppermute | solution.py:194
  292.5 41.7 %copy-start.1 = (s32[2,1024]{1,0:T(2,128)S(1)}, s32[2,1024]{1,0:T(2,128)}, u32[]{:S(2)}) copy-start(s32[2,1024]{1,0:T(2,128)} %param.8) | copy-start | bytes 24580
where the time goes:
time: 337 us; the launch traced here: 334 us
  Pallas kernels  205 us (61%)
  starting transfers between devices  49.4 us (15%)
  waiting for transfers between devices  40.8 us (12%)
  blocking collectives  24.9 us (7%)
  local copies, waits for them, and re-layouts  12.8 us (4%)
    pallas_call x4, Pallas kernels, scores_call(): pl.pallas_call(functools.partial(scores_kernel, steps, scale, first, extr...  108 us
    pallas_call x3, Pallas kernels, update_call(): pl.pallas_call(functools.partial(update_kernel, count, len(after), loss i...  86.2 us
    ppermute x31, starting transfers between devices, swap(): return lax.ppermute(x, 'feat', [(i, i ^ k) for i in range(8)])  47.4 us
    ppermute x31, waiting for transfers between devices, swap(): return lax.ppermute(x, 'feat', [(i, i ^ k) for i in range(8)])  40.7 us
    psum x2, blocking collectives, step(): lax.psum(sums, 'cls')  13.6 us
    unnamed x26, local copies, waits for them, and re-layouts  11.9 us
    psum x2, blocking collectives, step(): lax.psum(t, 'cls')  11.3 us
    pallas_call x12, Pallas kernels, small_call(): pl.pallas_call(body, grid_spec=pltpu.PrefetchScalarGridSpec(num_scalar_pr...  11.1 us
  transfers between devices with their start and end apart: 34, of which 8 were waited for; matrix products, arithmetic and copies ran while one was open for 0% of the time, Pallas kernels for 47%

commit v1 on v0

--- a/solution.py
+++ b/solution.py
@@ -273,7 +273,7 @@
 def spread(where, block, after, carry=()):
     line = [swap(block, k) for k in (2, 4, 6)]
     pair = swap(block, 1)
-    line, *carry = small_call(stack_kernel, where, line, [((3, *block.shape), bf16)], "line", (), after, carry)
+    line, *carry = small_call(stack_kernel, where, line, [((3, *block.shape), bf16)], "line", (), [*after, pair], carry)
     return [block, pair, line, swap(line, 1)], *carry
 
 

time: 337 us -> 336 us (level)
    ppermute x3, waiting for transfers between devices: 0.01 us -> 3.93 us  [over_cls(): lax.ppermute(x, 'cls', [(i, i ^ k) for i in range(4)])]
    unnamed x26 -> x22, local copies, waits for them, and re-layouts: 11.9 us -> 9.98 us
  transfers between devices with their start and end apart: 34 -> 34, of which waited for: 8 -> 7; matrix products, arithmetic and copies ran while one was open for 0% -> 0% of each run, Pallas kernels for 47% -> 47%
where the time goes in v1:
time: 336 us; the launch traced here: 335 us
  Pallas kernels  205 us (61%)
  starting transfers between devices  47.9 us (14%)
  waiting for transfers between devices  44.1 us (13%)
  blocking collectives  25.4 us (8%)
  local copies, waits for them, and re-layouts  10.9 us (3%)
    pallas_call x4, Pallas kernels, scores_call(): pl.pallas_call(functools.partial(scores_kernel, steps, scale, first, extr...  108 us
    pallas_call x3, Pallas kernels, update_call(): pl.pallas_call(functools.partial(update_kernel, count, len(after), loss i...  86.2 us
    ppermute x31, starting transfers between devices, swap(): return lax.ppermute(x, 'feat', [(i, i ^ k) for i in range(8)])  46 us
    ppermute x31, waiting for transfers between devices, swap(): return lax.ppermute(x, 'feat', [(i, i ^ k) for i in range(8)])  40.2 us
    psum x2, blocking collectives, step(): lax.psum(t, 'cls')  12.8 us
    psum x2, blocking collectives, step(): lax.psum(sums, 'cls')  12.6 us
    pallas_call x12, Pallas kernels, small_call(): pl.pallas_call(body, grid_spec=pltpu.PrefetchScalarGridSpec(num_scalar_pr...  11.1 us
    unnamed x22, local copies, waits for them, and re-layouts  9.98 us
  transfers between devices with their start and end apart: 34, of which 7 were waited for; matrix products, arithmetic and copies ran while one was open for 0% of the time, Pallas kernels for 47%

profile of v1, /device:TPU:0, one launch (start us, length us, event | category | flops | bytes accessed | tf_op | source)
XLA Modules:
  0.0 334.6 jit_solution(15836717746422138648)
XLA Ops:
  0.6 1.0 slice_bitcast_fusion
  1.6 3.0 collective-permute-start.6
  4.6 1.5 collective-permute-start.5
  6.2 3.9 %collective-permute-start.3 = (bf16[360,128]{1,0:T(8,128)(2,1)S(1)}, bf16[360,128]{1,0:T(8,128)(2,1)S(1)}, u32[]{:S(2)}, u32[]{:S(2)}) collective-permute-start(bf16[360,128]{1,0:T(8,128)(2,1)S(1)} %get-tuple-element.79.refs_1_), channel_id=1, source_target_pairs={{0,20},{4,16},{8,28},{12,24},{16,4},{20,0},{24,12},{28,8},{1,21},{... | collective-permute-start | bytes 276488 | tf_op jit(solution)/shard_map/ppermute | solution.py:194
  10.2 0.3 collective-permute-start.2
  10.5 3.5 %collective-permute-start.1 = (bf16[360,128]{1,0:T(8,128)(2,1)S(1)}, bf16[360,128]{1,0:T(8,128)(2,1)S(1)}, u32[]{:S(2)}, u32[]{:S(2)}) collective-permute-start(bf16[360,128]{1,0:T(8,128)(2,1)S(1)} %get-tuple-element.79.refs_1_), channel_id=1, source_target_pairs={{0,28},{4,24},{8,20},{12,16},{16,12},{20,8},{24,4},{28,0},{1,29},{... | collective-permute-start | bytes 276488 | tf_op jit(solution)/shard_map/ppermute | solution.py:194
  14.0 0.9 collective-permute-start
  15.0 0.9 collective-permute-start.8
  15.9 7.8 %collective-permute-done.2.refs_3_ = bf16[360,128]{1,0:T(8,128)(2,1)S(1)} collective-permute-done((bf16[360,128]{1,0:T(8,128)(2,1)S(1)}, bf16[360,128]{1,0:T(8,128)(2,1)S(1)}, u32[]{:S(2)}, u32[]{:S(2)}) %collective-permute-start.2) | collective-permute-done | bytes 92192 | tf_op jit(solution)/shard_map/ppermute | solution.py:194
  23.7 2.7 copy-done.2
  26.3 0.8 copy-done.9
  27.1 37.1 %features_scores.4 = (bf16[1024,8192]{1,0:T(8,128)(2,1)}, bf16[3,1264,128]{2,1,0:T(8,128)(2,1)S(1)}, f32[3,1264,128]{2,1,0:T(8,128)S(1)}, bf16[1264,8192]{1,0:T(8,128)(2,1)}, bf16[2,360,128]{2,1,0:T(8,128)(2,1)S(1)}) custom-call(s32[4]{0:T(128)S(1)} %pad_add_fusion.refs_0_.where_ref, bf16[360,128]{1,0:T(8,128)(2,1)S(1)} %collective-permute-done.refs_1_, ...), custom_call_target="tpu_custom_call" | custom-call | flops 20434649088 | bytes 33292288 | tf_op jit(solution)/shard_map/features_scores/pallas_call | solution.py:137
  64.2 0.6 collective-permute-start.11
  64.8 4.9 %collective-permute-start.10 = (bf16[2,360,128]{2,1,0:T(8,128)(2,1)S(1)}, bf16[2,360,128]{2,1,0:T(8,128)(2,1)S(1)}, u32[]{:S(2)}, u32[]{:S(2)}) collective-permute-start(bf16[2,360,128]{2,1,0:T(8,128)(2,1)S(1)} %get-tuple-element.40.refs_7_.refs_2_), channel_id=1, source_target_pairs={{0,16},{4,20},{8,24},{12,28},{16,0},{20,4},{24,8},{28,12},{1,17},{... | collective-permute-start | bytes 552968 | tf_op jit(solution)/shard_map/ppermute | solution.py:194
  69.6 1.0 collective-permute-start.9
  70.7 16.7 %features_scores.5 = (bf16[1024,8192]{1,0:T(8,128)(2,1)}, bf16[1,1264,128]{2,1,0:T(8,128)(2,1)S(1)}, f32[1,1264,128]{2,1,0:T(8,128)S(1)}) custom-call(s32[4]{0:T(128)S(1)} %pad_add_fusion.refs_0_.where_ref, bf16[360,128]{1,0:T(8,128)(2,1)S(1)} %get-tuple-element.79.refs_1_, ...), custom_call_target="tpu_custom_call", output_to_operand_aliasing={{0}: (6, {})} | custom-call | flops 6811549696 | bytes 24903680 | tf_op jit(solution)/shard_map/features_scores/pallas_call | solution.py:137
  87.4 0.8 pair_sums.3
  88.2 1.8 collective-permute-start.12
  89.9 3.2 collective-permute-start.14
  93.2 1.4 collective-permute-start.13
  94.6 27.2 %features_scores.6 = (bf16[1024,8192]{1,0:T(8,128)(2,1)}, bf16[2,1520,128]{2,1,0:T(8,128)(2,1)S(1)}, f32[2,1520,128]{2,1,0:T(8,128)S(1)}) custom-call(s32[4]{0:T(128)S(1)} %pad_add_fusion.refs_0_.where_ref, bf16[2,360,128]{2,1,0:T(8,128)(2,1)S(1)} %collective-permute-done.9.refs_4_.refs_1_, bf16[2,360,128]{2,1,0:T(8,128)(2,1)S(1)} %collective-permute-done.10.refs_5_.refs_2_, ...), custom_call_target="tpu_custom_call" | custom-call | flops 15770583040 | bytes 29097984 | tf_op jit(solution)/shard_map/features_scores/pallas_call | solution.py:137
  121.8 1.1 target.2
  122.9 1.8 collective-permute-start.16
  124.7 6.0 %psum.28.refs_3_ = f32[1,128]{1,0:T(1,128)S(1)} all-reduce(f32[1,128]{1,0:T(1,128)S(1)} %get-tuple-element.57), channel_id=1, replica_groups=mesh['feat'=8,'cls'=4] {'cls'}, use_global_device_ids=true, to_apply=%region_0.0 | all-reduce | flops 128 | bytes 1024 | tf_op jit(solution)/shard_map/psum | solution.py:378
  130.7 0.8 margin.2
  131.5 0.9 copy-done.5
  132.4 6.6 %psum.29.refs_3_ = f32[2,128]{1,0:T(2,128)S(1)} all-reduce(f32[2,128]{1,0:T(2,128)S(1)} %get-tuple-element.59), channel_id=1, replica_groups=mesh['feat'=8,'cls'=4] {'cls'}, use_global_device_ids=true, to_apply=%region_1.0 | all-reduce | flops 256 | bytes 2048 | tf_op jit(solution)/shard_map/psum | solution.py:385
  139.0 1.1 copy-done.6
  140.1 0.6 step_grad.2.refs_3_.refs_10_.refs_0_
  140.7 0.4 collective-permute-start.20
  141.1 2.4 collective-permute-start.19
  143.5 2.0 collective-permute-start.17
  145.5 1.8 pair_sums.4
  147.3 2.7 copy-done.4
  149.9 27.1 %features_scores.7 = (bf16[1024,8192]{1,0:T(8,128)(2,1)}, bf16[2,1520,128]{2,1,0:T(8,128)(2,1)S(1)}, f32[2,1520,128]{2,1,0:T(8,128)S(1)}) custom-call(s32[4]{0:T(128)S(1)} %pad_add_fusion.refs_0_.where_ref, bf16[2,360,128]{2,1,0:T(8,128)(2,1)S(1)} %collective-permute-done.7.refs_6_.refs_1_, ...), custom_call_target="tpu_custom_call", output_to_operand_aliasing={{0}: (7, {})} | custom-call | flops 15770583040 | bytes 29097984 | tf_op jit(solution)/shard_map/features_scores/pallas_call | solution.py:137
  177.0 0.6 line.2
  177.6 1.8 collective-permute-start.21
  179.7 1.1 collective-permute-start.23
  180.9 1.3 collective-permute-start.24
  182.1 15.9 %collective-permute-done.21.refs_2_ = bf16[2,1520,128]{2,1,0:T(8,128)(2,1)S(1)} collective-permute-done((bf16[2,1520,128]{2,1,0:T(8,128)(2,1)S(1)}, bf16[2,1520,128]{2,1,0:T(8,128)(2,1)S(1)}, u32[]{:S(2)}, u32[]{:S(2)}) %collective-permute-start.21) | collective-permute-done | bytes 778272 | tf_op jit(solution)/shard_map/ppermute | solution.py:194
  198.0 0.7 pair_sums.5
  198.8 6.7 %collective-permute-done.23.refs_3_ = bf16[1520,128]{1,0:T(8,128)(2,1)S(1)} collective-permute-done((bf16[1520,128]{1,0:T(8,128)(2,1)S(1)}, bf16[1520,128]{1,0:T(8,128)(2,1)S(1)}, u32[]{:S(2)}, u32[]{:S(2)}) %collective-permute-start.23) | collective-permute-done | bytes 389152 | tf_op jit(solution)/shard_map/ppermute | solution.py:194
  205.5 8.2 %collective-permute-done.22.refs_2_ = bf16[1520,128]{1,0:T(8,128)(2,1)S(1)} collective-permute-done((bf16[1520,128]{1,0:T(8,128)(2,1)S(1)}, bf16[1520,128]{1,0:T(8,128)(2,1)S(1)}, u32[]{:S(2)}, u32[]{:S(2)}) %collective-permute-start.22) | collective-permute-done | bytes 389152 | tf_op jit(solution)/shard_map/ppermute | solution.py:194
  213.7 0.6 gram.1.refs_6_
  214.3 1.1 collective-permute-start.27
  215.4 0.6 collective-permute-start.26
  216.2 2.3 collective-permute-done.27.refs_9_
  218.6 1.6 collective-permute-done.26.refs_8_
  220.2 2.1 target.3
  222.2 6.8 %psum.30.refs_3_ = f32[1,128]{1,0:T(1,128)S(1)} all-reduce(f32[1,128]{1,0:T(1,128)S(1)} %get-tuple-element.69), channel_id=1, replica_groups=mesh['feat'=8,'cls'=4] {'cls'}, use_global_device_ids=true, to_apply=%region_2.0 | all-reduce | flops 128 | bytes 1024 | tf_op jit(solution)/shard_map/psum | solution.py:378
  229.0 0.8 margin.3
  229.8 0.8 copy-done.7
  230.7 6.0 %psum.31.refs_3_ = f32[2,128]{1,0:T(2,128)S(1)} all-reduce(f32[2,128]{1,0:T(2,128)S(1)} %get-tuple-element.71), channel_id=1, replica_groups=mesh['feat'=8,'cls'=4] {'cls'}, use_global_device_ids=true, to_apply=%region_3.0 | all-reduce | flops 256 | bytes 2048 | tf_op jit(solution)/shard_map/psum | solution.py:385
  236.6 1.1 copy-done.8
  237.7 0.6 step_grad.3.refs_6_.refs_0_
  238.4 2.4 collective-permute-start.32
  240.8 2.0 collective-permute-start.30
  242.8 1.7 collective-permute-start.29
  244.5 22.3 %update.3 = (f32[1250,8192]{1,0:T(8,128)}, f32[1,2]{1,0:T(1,128)S(1)}) custom-call(s32[4]{0:T(128)S(1)} %pad_add_fusion.refs_0_.where_ref, bf16[1264,128]{1,0:T(8,128)(2,1)S(1)} %step_grad.2.refs_3_.refs_10_.refs_0_, bf16[1264,128]{1,0:T(8,128)(2,1)S(1)} %collective-permute-done.20.refs_5_.refs_11_.refs_1_, ...), custom_call_target="tpu_custom_call" | custom-call | flops 10603200512 | bytes 49807360 | tf_op jit(solution)/shard_map/update/pallas_call | solution.py:327
  266.7 1.6 collective-permute-done.31.refs_2_
  268.3 0.6 line.3.refs_7_.refs_2_
  268.9 1.7 collective-permute-start.33
  270.7 22.3 %update.4 = (f32[1250,8192]{1,0:T(8,128)}, f32[1,2]{1,0:T(1,128)}) custom-call(s32[4]{0:T(128)S(1)} %pad_add_fusion.refs_0_.where_ref, bf16[1264,128]{1,0:T(8,128)(2,1)S(1)} %step_grad.2.refs_3_.refs_10_.refs_0_, bf16[1264,128]{1,0:T(8,128)(2,1)S(1)} %collective-permute-done.20.refs_5_.refs_11_.refs_1_, ...), custom_call_target="tpu_custom_call", output_to_operand_aliasing={{0}: (7, {})} | custom-call | flops 10603200512 | bytes 49807360 | tf_op jit(solution)/shard_map/update/pallas_call | solution.py:327
  293.0 41.7 %update.5 = (f32[1250,8192]{1,0:T(8,128)}, f32[1,2]{1,0:T(1,128)}) custom-call(s32[4]{0:T(128)S(1)} %pad_add_fusion.refs_0_.where_ref, bf16[1264,128]{1,0:T(8,128)(2,1)S(1)} %step_grad.3.refs_6_.refs_0_, bf16[1264,128]{1,0:T(8,128)(2,1)S(1)} %collective-permute-done.29.refs_5_.refs_1_, ...), custom_call_target="tpu_custom_call", output_to_operand_aliasing={{0}: (6, {})} | custom-call | flops 21206401024 | bytes 99614720 | tf_op jit(solution)/shard_map/update/pallas_call | solution.py:327
  (53 shorter events, 0.9 us)
Async XLA Ops:
  0.6 64.1 %copy-start = (s32[2,1024]{1,0:T(2,128)S(1)}, s32[2,1024]{1,0:T(2,128)}, u32[]{:S(2)}) copy-start(s32[2,1024]{1,0:T(2,128)} %param.8) | copy-start | bytes 24580
  1.6 8.9 %collective-permute-start.6 = (bf16[360,128]{1,0:T(8,128)(2,1)S(1)}, bf16[360,128]{1,0:T(8,128)(2,1)S(1)}, u32[]{:S(2)}, u32[]{:S(2)}) collective-permute-start(bf16[360,128]{1,0:T(8,128)(2,1)S(1)} %get-tuple-element.78.refs_10_), channel_id=1, source_target_pairs={{0,4},{4,0},{8,12},{12,8},{16,20},{20,16},{24,28},{28,24},{1,5},{5... | collective-permute-start | bytes 276488 | tf_op jit(solution)/shard_map/ppermute | solution.py:194
  4.6 9.4 %collective-permute-start.5 = (bf16[360,128]{1,0:T(8,128)(2,1)S(1)}, bf16[360,128]{1,0:T(8,128)(2,1)S(1)}, u32[]{:S(2)}, u32[]{:S(2)}) collective-permute-start(bf16[360,128]{1,0:T(8,128)(2,1)S(1)} %get-tuple-element.79.refs_1_), channel_id=1, source_target_pairs={{0,12},{4,8},{8,4},{12,0},{16,28},{20,24},{24,20},{28,16},{1,13},{... | collective-permute-start | bytes 276488 | tf_op jit(solution)/shard_map/ppermute | solution.py:194
  6.2 8.8 %collective-permute-start.4 = (bf16[360,128]{1,0:T(8,128)(2,1)S(1)}, bf16[360,128]{1,0:T(8,128)(2,1)S(1)}, u32[]{:S(2)}, u32[]{:S(2)}) collective-permute-start(bf16[360,128]{1,0:T(8,128)(2,1)S(1)} %get-tuple-element.79.refs_1_), channel_id=1, source_target_pairs={{0,8},{4,12},{8,0},{12,4},{16,24},{20,28},{24,16},{28,20},{1,9},{5... | collective-permute-start | bytes 276488 | tf_op jit(solution)/shard_map/ppermute | solution.py:194
  6.2 9.7 %collective-permute-start.3 = (bf16[360,128]{1,0:T(8,128)(2,1)S(1)}, bf16[360,128]{1,0:T(8,128)(2,1)S(1)}, u32[]{:S(2)}, u32[]{:S(2)}) collective-permute-start(bf16[360,128]{1,0:T(8,128)(2,1)S(1)} %get-tuple-element.79.refs_1_), channel_id=1, source_target_pairs={{0,20},{4,16},{8,28},{12,24},{16,4},{20,0},{24,12},{28,8},{1,21},{... | collective-permute-start | bytes 276488 | tf_op jit(solution)/shard_map/ppermute | solution.py:194
  10.2 13.5 %collective-permute-start.2 = (bf16[360,128]{1,0:T(8,128)(2,1)S(1)}, bf16[360,128]{1,0:T(8,128)(2,1)S(1)}, u32[]{:S(2)}, u32[]{:S(2)}) collective-permute-start(bf16[360,128]{1,0:T(8,128)(2,1)S(1)} %get-tuple-element.79.refs_1_), channel_id=1, source_target_pairs={{0,16},{4,20},{8,24},{12,28},{16,0},{20,4},{24,8},{28,12},{1,17},{... | collective-permute-start | bytes 276488 | tf_op jit(solution)/shard_map/ppermute | solution.py:194
  10.5 13.2 %collective-permute-start.1 = (bf16[360,128]{1,0:T(8,128)(2,1)S(1)}, bf16[360,128]{1,0:T(8,128)(2,1)S(1)}, u32[]{:S(2)}, u32[]{:S(2)}) collective-permute-start(bf16[360,128]{1,0:T(8,128)(2,1)S(1)} %get-tuple-element.79.refs_1_), channel_id=1, source_target_pairs={{0,28},{4,24},{8,20},{12,16},{16,12},{20,8},{24,4},{28,0},{1,29},{... | collective-permute-start | bytes 276488 | tf_op jit(solution)/shard_map/ppermute | solution.py:194
  14.0 9.6 %collective-permute-start = (bf16[360,128]{1,0:T(8,128)(2,1)S(1)}, bf16[360,128]{1,0:T(8,128)(2,1)S(1)}, u32[]{:S(2)}, u32[]{:S(2)}) collective-permute-start(bf16[360,128]{1,0:T(8,128)(2,1)S(1)} %get-tuple-element.79.refs_1_), channel_id=1, source_target_pairs={{0,24},{4,28},{8,16},{12,20},{16,8},{20,12},{24,0},{28,4},{1,25},{... | collective-permute-start | bytes 276488 | tf_op jit(solution)/shard_map/ppermute | solution.py:194
  15.0 55.7 %collective-permute-start.8 = (bf16[360,128]{1,0:T(8,128)(2,1)S(1)}, bf16[360,128]{1,0:T(8,128)(2,1)S(1)}, u32[]{:S(2)}, u32[]{:S(2)}) collective-permute-start(bf16[360,128]{1,0:T(8,128)(2,1)S(1)} %get-tuple-element.79.refs_1_), channel_id=1, source_target_pairs={{0,4},{4,0},{8,12},{12,8},{16,20},{20,16},{24,28},{28,24},{1,5},{5... | collective-permute-start | bytes 276488 | tf_op jit(solution)/shard_map/ppermute | solution.py:194
  23.6 2.7 copy-start.2
  26.3 0.8 copy-start.9
  27.1 43.6 %copy-start.3 = (bf16[360,8192]{1,0:T(8,128)(2,1)S(1)}, bf16[360,8192]{1,0:T(8,128)(2,1)}, u32[]{:S(2)}) copy-start(bf16[360,8192]{1,0:T(8,128)(2,1)} %refs_3_.5) | copy-start | bytes 17694724
  64.2 23.2 %collective-permute-start.11 = (bf16[3,1264,128]{2,1,0:T(8,128)(2,1)S(1)}, bf16[3,1264,128]{2,1,0:T(8,128)(2,1)S(1)}, u32[]{:S(2)}, u32[]{:S(2)}) collective-permute-start(bf16[3,1264,128]{2,1,0:T(8,128)(2,1)S(1)} %get-tuple-element.45), channel_id=1, source_target_pairs={{0,4},{4,0},{8,12},{12,8},{16,20},{20,16},{24,28},{28,24},{1,5},{5... | collective-permute-start | bytes 2912264 | tf_op jit(solution)/shard_map/ppermute | solution.py:194
  64.8 22.6 %collective-permute-start.10 = (bf16[2,360,128]{2,1,0:T(8,128)(2,1)S(1)}, bf16[2,360,128]{2,1,0:T(8,128)(2,1)S(1)}, u32[]{:S(2)}, u32[]{:S(2)}) collective-permute-start(bf16[2,360,128]{2,1,0:T(8,128)(2,1)S(1)} %get-tuple-element.40.refs_7_.refs_2_), channel_id=1, source_target_pairs={{0,16},{4,20},{8,24},{12,28},{16,0},{20,4},{24,8},{28,12},{1,17},{... | collective-permute-start | bytes 552968 | tf_op jit(solution)/shard_map/ppermute | solution.py:194
  69.6 17.7 %collective-permute-start.9 = (bf16[2,360,128]{2,1,0:T(8,128)(2,1)S(1)}, bf16[2,360,128]{2,1,0:T(8,128)(2,1)S(1)}, u32[]{:S(2)}, u32[]{:S(2)}) collective-permute-start(bf16[2,360,128]{2,1,0:T(8,128)(2,1)S(1)} %get-tuple-element.40.refs_7_.refs_2_), channel_id=1, source_target_pairs={{0,24},{4,28},{8,16},{12,20},{16,8},{20,12},{24,0},{28,4},{1,25},{... | collective-permute-start | bytes 552968 | tf_op jit(solution)/shard_map/ppermute | solution.py:194
  70.6 16.7 %collective-permute-start.7 = (bf16[2,360,128]{2,1,0:T(8,128)(2,1)S(1)}, bf16[2,360,128]{2,1,0:T(8,128)(2,1)S(1)}, u32[]{:S(2)}, u32[]{:S(2)}) collective-permute-start(bf16[2,360,128]{2,1,0:T(8,128)(2,1)S(1)} %get-tuple-element.40.refs_7_.refs_2_), channel_id=1, source_target_pairs={{0,8},{4,12},{8,0},{12,4},{16,24},{20,28},{24,16},{28,20},{1,9},{5... | collective-permute-start | bytes 552968 | tf_op jit(solution)/shard_map/ppermute | solution.py:194
  70.6 24.0 %copy-start.10 = (s32[8192]{0:T(1024)S(1)}, s32[8192]{0:T(1024)}, u32[]{:S(2)}) copy-start(s32[8192]{0:T(1024)} %param.7) | copy-start | bytes 98308
  88.2 33.6 %collective-permute-start.12 = (bf16[1,1264,128]{2,1,0:T(8,128)(2,1)S(1)}, bf16[1,1264,128]{2,1,0:T(8,128)(2,1)S(1)}, u32[]{:S(2)}, u32[]{:S(2)}) collective-permute-start(bf16[1,1264,128]{2,1,0:T(8,128)(2,1)S(1)} %get-tuple-element.51), channel_id=1, source_target_pairs={{0,4},{4,0},{8,12},{12,8},{16,20},{20,16},{24,28},{28,24},{1,5},{5... | collective-permute-start | bytes 970760 | tf_op jit(solution)/shard_map/ppermute | solution.py:194
  89.9 31.9 %collective-permute-start.14 = (bf16[1264,128]{1,0:T(8,128)(2,1)S(1)}, bf16[1264,128]{1,0:T(8,128)(2,1)S(1)}, u32[]{:S(2)}, u32[]{:S(2)}) collective-permute-start(bf16[1264,128]{1,0:T(8,128)(2,1)S(1)} %get-tuple-element.52), channel_id=1, source_target_pairs={{0,16},{4,20},{8,24},{12,28},{16,0},{20,4},{24,8},{28,12},{1,17},{... | collective-permute-start | bytes 970760 | tf_op jit(solution)/shard_map/ppermute | solution.py:194
  93.1 28.7 %collective-permute-start.15 = (bf16[1264,128]{1,0:T(8,128)(2,1)S(1)}, bf16[1264,128]{1,0:T(8,128)(2,1)S(1)}, u32[]{:S(2)}, u32[]{:S(2)}) collective-permute-start(bf16[1264,128]{1,0:T(8,128)(2,1)S(1)} %get-tuple-element.53), channel_id=1, source_target_pairs={{0,8},{4,12},{8,0},{12,4},{16,24},{20,28},{24,16},{28,20},{1,9},{5... | collective-permute-start | bytes 970760 | tf_op jit(solution)/shard_map/ppermute | solution.py:194
  93.2 28.7 %collective-permute-start.13 = (bf16[1264,128]{1,0:T(8,128)(2,1)S(1)}, bf16[1264,128]{1,0:T(8,128)(2,1)S(1)}, u32[]{:S(2)}, u32[]{:S(2)}) collective-permute-start(bf16[1264,128]{1,0:T(8,128)(2,1)S(1)} %get-tuple-element.48.refs_7_), channel_id=1, source_target_pairs={{0,24},{4,28},{8,16},{12,20},{16,8},{20,12},{24,0},{28,4},{1,25},{... | collective-permute-start | bytes 970760 | tf_op jit(solution)/shard_map/ppermute | solution.py:194
  122.9 22.6 %collective-permute-start.16 = (bf16[2,1520,128]{2,1,0:T(8,128)(2,1)S(1)}, bf16[2,1520,128]{2,1,0:T(8,128)(2,1)}, u32[]{:S(2)}, u32[]{:S(2)}) collective-permute-start(bf16[2,1520,128]{2,1,0:T(8,128)(2,1)S(1)} %get-tuple-element.55), channel_id=1, source_target_pairs={{0,4},{4,0},{8,12},{12,8},{16,20},{20,16},{24,28},{28,24},{1,5},{5... | collective-permute-start | bytes 2334728 | tf_op jit(solution)/shard_map/ppermute | solution.py:194
  131.5 0.9 copy-start.5
  139.0 1.1 copy-start.6
  140.7 36.3 %collective-permute-start.20 = (bf16[1264,128]{1,0:T(8,128)(2,1)S(1)}, bf16[1264,128]{1,0:T(8,128)(2,1)S(1)}, u32[]{:S(2)}, u32[]{:S(2)}) collective-permute-start(bf16[1264,128]{1,0:T(8,128)(2,1)S(1)} %step_grad.2.refs_3_.refs_10_.refs_0_), channel_id=1, source_target_pairs={{0,4},{4,0},{8,12},{12,8},{16,20},{20,16},{24,28},{28,24},{1,5},{5... | collective-permute-start | bytes 970760 | tf_op jit(solution)/shard_map/ppermute | solution.py:194
  141.1 35.9 %collective-permute-start.19 = (bf16[1264,128]{1,0:T(8,128)(2,1)S(1)}, bf16[1264,128]{1,0:T(8,128)(2,1)S(1)}, u32[]{:S(2)}, u32[]{:S(2)}) collective-permute-start(bf16[1264,128]{1,0:T(8,128)(2,1)S(1)} %step_grad.2.refs_3_.refs_10_.refs_0_), channel_id=1, source_target_pairs={{0,24},{4,28},{8,16},{12,20},{16,8},{20,12},{24,0},{28,4},{1,25},{... | collective-permute-start | bytes 970760 | tf_op jit(solution)/shard_map/ppermute | solution.py:194
  143.5 33.6 %collective-permute-start.18 = (bf16[1264,128]{1,0:T(8,128)(2,1)S(1)}, bf16[1264,128]{1,0:T(8,128)(2,1)S(1)}, u32[]{:S(2)}, u32[]{:S(2)}) collective-permute-start(bf16[1264,128]{1,0:T(8,128)(2,1)S(1)} %step_grad.2.refs_3_.refs_10_.refs_0_), channel_id=1, source_target_pairs={{0,16},{4,20},{8,24},{12,28},{16,0},{20,4},{24,8},{28,12},{1,17},{... | collective-permute-start | bytes 970760 | tf_op jit(solution)/shard_map/ppermute | solution.py:194
  143.5 33.6 %collective-permute-start.17 = (bf16[1264,128]{1,0:T(8,128)(2,1)S(1)}, bf16[1264,128]{1,0:T(8,128)(2,1)S(1)}, u32[]{:S(2)}, u32[]{:S(2)}) collective-permute-start(bf16[1264,128]{1,0:T(8,128)(2,1)S(1)} %step_grad.2.refs_3_.refs_10_.refs_0_), channel_id=1, source_target_pairs={{0,8},{4,12},{8,0},{12,4},{16,24},{20,28},{24,16},{28,20},{1,9},{5... | collective-permute-start | bytes 970760 | tf_op jit(solution)/shard_map/ppermute | solution.py:194
  147.3 2.7 copy-start.4
  177.6 20.4 %collective-permute-start.21 = (bf16[2,1520,128]{2,1,0:T(8,128)(2,1)S(1)}, bf16[2,1520,128]{2,1,0:T(8,128)(2,1)S(1)}, u32[]{:S(2)}, u32[]{:S(2)}) collective-permute-start(bf16[2,1520,128]{2,1,0:T(8,128)(2,1)S(1)} %get-tuple-element.63), channel_id=1, source_target_pairs={{0,4},{4,0},{8,12},{12,8},{16,20},{20,16},{24,28},{28,24},{1,5},{5... | collective-permute-start | bytes 2334728 | tf_op jit(solution)/shard_map/ppermute | solution.py:194
  179.5 36.8 %collective-permute-start.28 = (bf16[3,1264,128]{2,1,0:T(8,128)(2,1)S(1)}, bf16[3,1264,128]{2,1,0:T(8,128)(2,1)S(1)}, u32[]{:S(2)}, u32[]{:S(2)}) collective-permute-start(bf16[3,1264,128]{2,1,0:T(8,128)(2,1)S(1)} %get-tuple-element.64.refs_3_.refs_12_.refs_2_), channel_id=1, source_target_pairs={{0,4},{4,0},{8,12},{12,8},{16,20},{20,16},{24,28},{28,24},{1,5},{5... | collective-permute-start | bytes 2912264 | tf_op jit(solution)/shard_map/ppermute | solution.py:194
  179.7 25.8 %collective-permute-start.23 = (bf16[1520,128]{1,0:T(8,128)(2,1)S(1)}, bf16[1520,128]{1,0:T(8,128)(2,1)S(1)}, u32[]{:S(2)}, u32[]{:S(2)}) collective-permute-start(bf16[1520,128]{1,0:T(8,128)(2,1)S(1)} %get-tuple-element.60.refs_8_), channel_id=1, source_target_pairs={{0,16},{4,20},{8,24},{12,28},{16,0},{20,4},{24,8},{28,12},{1,17},{... | collective-permute-start | bytes 1167368 | tf_op jit(solution)/shard_map/ppermute | solution.py:194
  180.9 17.9 %collective-permute-start.24 = (bf16[1520,128]{1,0:T(8,128)(2,1)S(1)}, bf16[1520,128]{1,0:T(8,128)(2,1)S(1)}, u32[]{:S(2)}, u32[]{:S(2)}) collective-permute-start(bf16[1520,128]{1,0:T(8,128)(2,1)S(1)} %get-tuple-element.67), channel_id=1, source_target_pairs={{0,24},{4,28},{8,16},{12,20},{16,8},{20,12},{24,0},{28,4},{1,25},{... | collective-permute-start | bytes 1167368 | tf_op jit(solution)/shard_map/ppermute | solution.py:194
  198.7 15.0 %collective-permute-start.22 = (bf16[1520,128]{1,0:T(8,128)(2,1)S(1)}, bf16[1520,128]{1,0:T(8,128)(2,1)S(1)}, u32[]{:S(2)}, u32[]{:S(2)}) collective-permute-start(bf16[1520,128]{1,0:T(8,128)(2,1)S(1)} %get-tuple-element.66), channel_id=1, source_target_pairs={{0,8},{4,12},{8,0},{12,4},{16,24},{20,28},{24,16},{28,20},{1,9},{5... | collective-permute-start | bytes 1167368 | tf_op jit(solution)/shard_map/ppermute | solution.py:194
  214.3 4.3 %collective-permute-start.27 = (bf16[256,128]{1,0:T(8,128)(2,1)S(1)}, bf16[256,128]{1,0:T(8,128)(2,1)S(1)}, u32[]{:S(2)}, u32[]{:S(2)}) collective-permute-start(bf16[256,128]{1,0:T(8,128)(2,1)S(1)} %gram.1.refs_6_), channel_id=1, source_target_pairs={{0,3},{1,2},{2,1},{3,0},{4,7},{5,6},{6,5},{7,4},{8,11},{9,10},{10,... | collective-permute-start | bytes 196616 | tf_op jit(solution)/shard_map/ppermute | solution.py:203
  215.4 4.8 %collective-permute-start.26 = (bf16[256,128]{1,0:T(8,128)(2,1)S(1)}, bf16[256,128]{1,0:T(8,128)(2,1)S(1)}, u32[]{:S(2)}, u32[]{:S(2)}) collective-permute-start(bf16[256,128]{1,0:T(8,128)(2,1)S(1)} %gram.1.refs_6_), channel_id=1, source_target_pairs={{0,2},{1,3},{2,0},{3,1},{4,6},{5,7},{6,4},{7,5},{8,10},{9,11},{10,... | collective-permute-start | bytes 196616 | tf_op jit(solution)/shard_map/ppermute | solution.py:203
  216.0 4.2 %collective-permute-start.25 = (bf16[256,128]{1,0:T(8,128)(2,1)S(1)}, bf16[256,128]{1,0:T(8,128)(2,1)S(1)}, u32[]{:S(2)}, u32[]{:S(2)}) collective-permute-start(bf16[256,128]{1,0:T(8,128)(2,1)S(1)} %gram.1.refs_6_), channel_id=1, source_target_pairs={{0,1},{1,0},{2,3},{3,2},{4,5},{5,4},{6,7},{7,6},{8,9},{9,8},{10,11... | collective-permute-start | bytes 196616 | tf_op jit(solution)/shard_map/ppermute | solution.py:203
  229.8 0.8 copy-start.7
  236.6 1.1 copy-start.8
  238.4 28.4 %collective-permute-start.32 = (bf16[1264,128]{1,0:T(8,128)(2,1)S(1)}, bf16[1264,128]{1,0:T(8,128)(2,1)S(1)}, u32[]{:S(2)}, u32[]{:S(2)}) collective-permute-start(bf16[1264,128]{1,0:T(8,128)(2,1)S(1)} %step_grad.3.refs_6_.refs_0_), channel_id=1, source_target_pairs={{0,24},{4,28},{8,16},{12,20},{16,8},{20,12},{24,0},{28,4},{1,25},{... | collective-permute-start | bytes 970760 | tf_op jit(solution)/shard_map/ppermute | solution.py:194
  240.8 27.5 %collective-permute-start.31 = (bf16[1264,128]{1,0:T(8,128)(2,1)S(1)}, bf16[1264,128]{1,0:T(8,128)(2,1)S(1)}, u32[]{:S(2)}, u32[]{:S(2)}) collective-permute-start(bf16[1264,128]{1,0:T(8,128)(2,1)S(1)} %step_grad.3.refs_6_.refs_0_), channel_id=1, source_target_pairs={{0,16},{4,20},{8,24},{12,28},{16,0},{20,4},{24,8},{28,12},{1,17},{... | collective-permute-start | bytes 970760 | tf_op jit(solution)/shard_map/ppermute | solution.py:194
  240.8 27.5 %collective-permute-start.30 = (bf16[1264,128]{1,0:T(8,128)(2,1)S(1)}, bf16[1264,128]{1,0:T(8,128)(2,1)S(1)}, u32[]{:S(2)}, u32[]{:S(2)}) collective-permute-start(bf16[1264,128]{1,0:T(8,128)(2,1)S(1)} %step_grad.3.refs_6_.refs_0_), channel_id=1, source_target_pairs={{0,8},{4,12},{8,0},{12,4},{16,24},{20,28},{24,16},{28,20},{1,9},{5... | collective-permute-start | bytes 970760 | tf_op jit(solution)/shard_map/ppermute | solution.py:194
  242.8 25.5 %collective-permute-start.29 = (bf16[1264,128]{1,0:T(8,128)(2,1)S(1)}, bf16[1264,128]{1,0:T(8,128)(2,1)S(1)}, u32[]{:S(2)}, u32[]{:S(2)}) collective-permute-start(bf16[1264,128]{1,0:T(8,128)(2,1)S(1)} %step_grad.3.refs_6_.refs_0_), channel_id=1, source_target_pairs={{0,4},{4,0},{8,12},{12,8},{16,20},{20,16},{24,28},{28,24},{1,5},{5... | collective-permute-start | bytes 970760 | tf_op jit(solution)/shard_map/ppermute | solution.py:194
  268.9 24.0 %collective-permute-start.33 = (bf16[3,1264,128]{2,1,0:T(8,128)(2,1)S(1)}, bf16[3,1264,128]{2,1,0:T(8,128)(2,1)S(1)}, u32[]{:S(2)}, u32[]{:S(2)}) collective-permute-start(bf16[3,1264,128]{2,1,0:T(8,128)(2,1)S(1)} %line.3.refs_7_.refs_2_), channel_id=1, source_target_pairs={{0,4},{4,0},{8,12},{12,8},{16,20},{20,16},{24,28},{28,24},{1,5},{5... | collective-permute-start | bytes 2912264 | tf_op jit(solution)/shard_map/ppermute | solution.py:194
  293.0 41.7 %copy-start.1 = (s32[2,1024]{1,0:T(2,128)S(1)}, s32[2,1024]{1,0:T(2,128)}, u32[]{:S(2)}) copy-start(s32[2,1024]{1,0:T(2,128)} %param.8) | copy-start | bytes 24580
